TPU v7x, 32 devices: a whole 2x2x4 slice. The times are simulated.
32 devices in a mesh: sector: 8 (over z, x), tile: 4 (over y, core).
Axes of the slice: x: 2, y: 2, z: 4, core: 2. Of those that a mesh axis runs over, the one named last changes fastest.
Arguments:
- rates: bfloat16 [16384, 1024], P(('sector', 'tile')), may hold values from -6 to 6
- target: bfloat16 [16384, 1024], P(('sector', 'tile')), may hold values from -6 to 6
- prior_consensus: float32 [16384, 1024], P(('sector', 'tile')), may hold values from -6 to 6
- duals: float32 [16384, 1024], P(('sector', 'tile')), may hold values from -6 to 6
- response: bfloat16 [16384, 512], P(('sector', 'tile')), may hold values from -0.25 to 0.25
- block_cols: int32 [128, 4], P(('sector', 'tile')), may hold values from 0 to 15, all different within a row
- slot_well: int32 [16384], P(('sector', 'tile')), may hold values from -1 to 1535, as said below
- well_owner: int32 [1536], replicated, may hold values from 0 to 31, as said below
Outputs:
- new_rates: bfloat16 [16384, 1024], P(('sector', 'tile'))
- new_duals: float32 [16384, 1024], P(('sector', 'tile'))
- consensus: float32 [16384, 1024], P(('sector', 'tile'))
Inputs may be any that keep to these rules, and one draw needn't show every extreme that they name: `block_cols`: each row names 4 different column blocks. `well_owner`: each device owns exactly 48 wells. `slot_well`: every well has exactly one slot on its owner device and at most one slot in each other sector, always on a device with the owner's tile index. The slots of one device holding wells owned in one other sector number at most 4; in every draw each device reaches 4 toward some sector, and some sector receives 4 from every other sector of each tile index.
All inputs are finite; a program needn't handle non-finite values.
Results may differ from a plain program's by a relative error of at most 0.0044.
Values may be sent and summed in bfloat16 or wider, within the bound.
A program may use at most 128 MiB of HBM per device.

v0:
```python
import jax
import jax.numpy as jnp
from jax import lax
from jax.sharding import PartitionSpec as P

NB = 4
INNER = 3
CAP = 4


def owner_ranks(well_owner, per_owner):
    sorting = jnp.argsort(well_owner, stable=True)
    placement = jnp.arange(well_owner.shape[0], dtype=jnp.int32) - well_owner[sorting] * per_owner
    return jnp.zeros_like(well_owner).at[sorting].set(placement)


def dense_coefficients(response, block_cols, sector_blocks):
    slot_count = response.shape[0]
    row_blocks = slot_count // 128
    coefficients = response.reshape(row_blocks, 128, NB, 128)
    selector = (block_cols[:, :, None] == jnp.arange(sector_blocks)[None, None, :]).astype(
        jnp.bfloat16
    )
    spread = jnp.einsum(
        "bikj,bkc->bicj", coefficients, selector, preferred_element_type=jnp.float32
    )
    return spread.astype(jnp.bfloat16).reshape(slot_count, sector_blocks * 128)


def shards(rates, target, prior_consensus, duals, response, block_cols, slot_well, well_owner):
    slot_count, periods = rates.shape
    sector_count = lax.axis_size("sector")
    tile_count = lax.axis_size("tile")
    per_owner = well_owner.shape[0] // (sector_count * tile_count)
    sector_blocks = tile_count * slot_count // 128
    expanded = dense_coefficients(response, block_cols, sector_blocks)
    pulled = 0.5 * (prior_consensus - duals)
    target_wide = target.astype(jnp.float32)
    iterate = rates
    for iteration in range(INNER):
        whole = lax.all_gather(iterate, "tile", axis=0, tiled=True)
        drawdown = jnp.dot(expanded, whole, preferred_element_type=jnp.float32)
        iterate = (
            (iterate.astype(jnp.float32) + 0.5 * (target_wide - drawdown) + pulled) / 1.5
        ).astype(jnp.bfloat16)
    rates_wide = iterate.astype(jnp.float32)
    offered = (rates_wide + duals).astype(jnp.bfloat16)
    self_index = lax.axis_index("sector") * tile_count + lax.axis_index("tile")
    shared = slot_well >= 0
    well_ids = jnp.maximum(slot_well, 0)
    owner_dev = well_owner[well_ids]
    owner_rank = owner_ranks(well_owner, per_owner)[well_ids]
    home_slot = shared & (owner_dev == self_index)
    outgoing = shared & (owner_dev != self_index)
    target_sector = owner_dev // tile_count
    bound_for = (
        (target_sector[:, None] == jnp.arange(sector_count)[None, :]) & outgoing[:, None]
    ).astype(jnp.int32)
    position = jnp.sum((jnp.cumsum(bound_for, axis=0) - bound_for) * bound_for, axis=1)
    buffer_rows = sector_count * CAP
    slot_index = jnp.where(outgoing, target_sector * CAP + position, buffer_rows)
    placing = (jnp.arange(buffer_rows)[:, None] == slot_index[None, :]).astype(jnp.bfloat16)
    send_values = jnp.dot(placing, offered, preferred_element_type=jnp.float32).astype(jnp.bfloat16)
    occupied = jnp.sum(placing.astype(jnp.float32), axis=1)
    rank_sum = jnp.dot(placing, owner_rank.astype(jnp.bfloat16), preferred_element_type=jnp.float32)
    send_ranks = (rank_sum + occupied - 1.0).astype(jnp.bfloat16)
    got_values, got_ranks = (
        lax.all_to_all(
            send_values.reshape(sector_count, CAP, periods),
            "sector",
            split_axis=0,
            concat_axis=0,
            tiled=True,
        ),
        lax.all_to_all(
            send_ranks.reshape(sector_count, CAP), "sector", split_axis=0, concat_axis=0, tiled=True
        ),
    )
    received = got_values.reshape(buffer_rows, periods)
    received_rank = got_ranks.reshape(buffer_rows).astype(jnp.float32)
    owned_slots = jnp.arange(per_owner)
    pick_received = (owned_slots.astype(jnp.float32)[:, None] == received_rank[None, :]).astype(
        jnp.bfloat16
    )
    pick_home = ((owned_slots[:, None] == owner_rank[None, :]) & home_slot[None, :]).astype(
        jnp.bfloat16
    )
    totals = jnp.dot(pick_received, received, preferred_element_type=jnp.float32)
    totals = totals + 2.0 * jnp.dot(pick_home, offered, preferred_element_type=jnp.float32)
    weight_sum = jnp.sum(pick_received.astype(jnp.float32), axis=1) + 2.0 * jnp.sum(
        pick_home.astype(jnp.float32), axis=1
    )
    owner_mean = totals / weight_sum[:, None]
    answer_rows = jnp.clip(received_rank.astype(jnp.int32), 0, per_owner - 1)
    answers = jnp.take(owner_mean, answer_rows, axis=0).reshape(sector_count, CAP, periods)
    returned = (
        lax.all_to_all(
            answers.astype(jnp.bfloat16), "sector", split_axis=0, concat_axis=0, tiled=True
        )
        .astype(answers.dtype)
        .reshape(buffer_rows, periods)
    )
    from_home = jnp.take(owner_mean, owner_rank, axis=0)
    from_peer = jnp.take(returned, jnp.clip(slot_index, 0, buffer_rows - 1), axis=0)
    slot_mean = jnp.where(home_slot[:, None], from_home, from_peer)
    consensus = jnp.where(shared[:, None], slot_mean, rates_wide)
    new_duals = jnp.where(shared[:, None], duals + rates_wide - consensus, duals)
    return (iterate, new_duals, consensus)


def solution(mesh):
    in_specs = (
        P(("sector", "tile"), None),
        P(("sector", "tile"), None),
        P(("sector", "tile"), None),
        P(("sector", "tile"), None),
        P(("sector", "tile"), None),
        P(("sector", "tile"), None),
        P(("sector", "tile")),
        P(),
    )
    out_specs = (
        P(("sector", "tile"), None),
        P(("sector", "tile"), None),
        P(("sector", "tile"), None),
    )
    return jax.shard_map(shards, mesh=mesh, in_specs=in_specs, out_specs=out_specs, check_vma=False)
```

profile of v0, /device:TPU:0, one launch (start us, length us, event | category | flops | bytes accessed | tf_op | source)
XLA Modules:
  0.0 185.4 jit_solution(885928451271018021)
XLA Ops:
  7.2 0.0 all-gather.4.cloned.1.call-start
  7.2 0.7 all-gather.4.cloned.1.call-update
  7.9 0.0 all-gather.6.cloned.1.call-start
  8.0 1.3 reshape.165
  9.3 2.4 %convolution_convert_fusion = bf16[4,16,128,128]{3,1,2,0:T(8,128)(2,1)} fusion(bf16[4,128,4,128]{3,2,1,0:T(4,128)(2,1)S(1)} %reshape.165, s32[4,4]{1,0:T(4,128)S(1)} %copy-done.8), kind=kOutput, calls=%fused_computation.35 | convolution fusion | flops 9437440 | bytes 2621504 | tf_op jit(solution)/shard_map/bikj,bkc->bicj/dot_general | solution.py:24
  11.7 35.1 %all-gather.4.cloned.1.call-done = bf16[2048,1024]{1,0:T(8,128)(2,1)} async-done(((bf16[512,1024]{1,0:T(8,128)(2,1)}), bf16[2048,1024]{1,0:T(8,128)(2,1)}) %all-gather.4.cloned.1.call-update) | async-done | bytes 4194320 | tf_op jit(solution)/shard_map/all_gather | solution.py:41
  46.8 7.8 %fusion.4 = bf16[512,1024]{1,0:T(8,128)(2,1)} fusion(bf16[512,1024]{1,0:T(8,128)(2,1)} %param.9, bf16[512,1024]{1,0:T(8,128)(2,1)} %param.8, bf16[2048,1024]{1,0:T(8,128)(2,1)} %all-gather.4.cloned.1.call-done, bf16[64,8,16,128]{3,2,1,0:T(8,128)(2,1)} %bitcast.68, f32[512,1024]{1,0:T(8,128)} %param.10, f32[512,1024]{1,0:T(8,128)S(1)} %copy-done.1), kind=kOutput, calls=%fused_computation.16 | convolution fusion | flops 2152726528 | bytes 13631488 | tf_op jit(solution)/shard_map/dot_general | solution.py:42
  54.7 0.0 all-gather.8.cloned.1.call-start
  54.7 34.6 %all-gather.6.cloned.1.call-done = bf16[2048,1024]{1,0:T(8,128)(2,1)} async-done(((bf16[512,1024]{1,0:T(8,128)(2,1)}), bf16[2048,1024]{1,0:T(8,128)(2,1)}) %all-gather.6.cloned.1.call-update) | async-done | bytes 4194320 | tf_op jit(solution)/shard_map/all_gather | solution.py:41
  89.3 7.5 %fusion.9 = bf16[512,1024]{1,0:T(8,128)(2,1)} fusion(bf16[512,1024]{1,0:T(8,128)(2,1)S(1)} %copy-done.10, bf16[512,1024]{1,0:T(8,128)(2,1)} %fusion.4, bf16[2048,1024]{1,0:T(8,128)(2,1)} %all-gather.6.cloned.1.call-done, bf16[64,8,16,128]{3,2,1,0:T(8,128)(2,1)} %bitcast.69, f32[512,1024]{1,0:T(8,128)} %param.10, f32[512,1024]{1,0:T(8,128)S(1)} %copy-done.1), kind=kOutput, calls=%fused_computation.21 | convolution fusion | flops 2152726528 | bytes 13631488 | tf_op jit(solution)/shard_map/dot_general | solution.py:42
  96.8 0.6 copy-done
  97.5 3.1 %gather_fusion = s32[512]{0:T(512)S(1)} fusion(s32[1536]{0:T(1024)S(1)} %copy-done, s32[1024]{0:T(1024)S(1)} %pad_clamp_fusion.4), kind=kCustom, calls=%fused_computation | custom fusion | bytes 6144 | tf_op jit(solution)/shard_map/gather | solution.py:51
  100.6 5.0 %sort.17 = (s32[1536]{0:T(1024)}, s32[1536]{0:T(1024)S(1)}) sort(s32[1536]{0:T(1024)S(1)} %copy-done, s32[1536]{0:T(1024)S(1)} %iota.31), dimensions={0}, to_apply=%region_0.0 | sort | flops 16896 | bytes 24576 | tf_op jit(solution)/shard_map/jit(argsort)/sort | solution.py:12
  105.7 8.4 %gather_fusion.1 = s32[1536]{0:T(1024)S(1)} fusion(s32[1536]{0:T(1024)S(1)} %copy-done, s32[2048]{0:T(1024)S(1)} %pad_clamp_fusion), kind=kCustom, calls=%fused_computation.1 | custom fusion | bytes 18432 | tf_op jit(solution)/shard_map/gather | solution.py:13
  114.1 6.2 %scatter_custom_fusion = s32[1536]{0:T(1024)S(1)} fusion(s32[1536]{0:T(1024)S(1)} %compare_select_fusion, s32[1536]{0:T(1024)S(1)} %multiply_subtract_fusion, s32[]{:T(128)} %constant.54.clone.1), kind=kCustom, calls=%fused_computation.90 | custom fusion | bytes 6148 | tf_op jit(solution)/shard_map/scatter | solution.py:14
  120.3 3.1 %gather_fusion.2 = s32[512]{0:T(512)S(1)} fusion(s32[1536]{0:T(1024)S(1)} %scatter_custom_fusion, s32[1024]{0:T(1024)S(1)} %pad_clamp_fusion.4), kind=kCustom, calls=%fused_computation.2 | custom fusion | bytes 6144 | tf_op jit(solution)/shard_map/gather | solution.py:52
  123.5 1.1 reduce-window.6
  124.6 0.2 slice_reduce_fusion
  124.9 0.1 fusion.45
  125.0 0.6 compare_and_fusion.1
  125.6 0.1 convert_reduce_fusion.1
  125.7 0.1 fusion.34
  125.8 0.7 all_to_all.16
  126.5 5.5 %all-to-all-start = ((bf16[8,1,4]{2,1,0:T(2,128)(2,1)}), bf16[8,1,4]{2,1,0:T(2,128)(2,1)S(1)}, u32[]{:S(2)}, u32[]{:S(2)}) async-start(bf16[8,1,4]{2,1,0:T(2,128)(2,1)} %all_to_all.16), calls=%async_computation | async-start | bytes 8192 | tf_op jit(solution)/shard_map/all_to_all | solution.py:75
  132.0 0.1 convert_reduce_fusion
  132.1 0.6 compare_and_fusion.3
  132.8 5.6 %all-to-all-done = bf16[8,1,4]{2,1,0:T(2,128)(2,1)S(1)} async-done(((bf16[8,1,4]{2,1,0:T(2,128)(2,1)}), bf16[8,1,4]{2,1,0:T(2,128)(2,1)S(1)}, u32[]{:S(2)}, u32[]{:S(2)}) %all-to-all-start) | async-done | bytes 96 | tf_op jit(solution)/shard_map/all_to_all | solution.py:75
  138.4 0.1 reshape.172
  138.5 0.1 min.28
  138.6 0.1 copy.19
  138.7 0.7 copy.20
  139.4 0.1 convert_reduce_fusion.2
  139.5 0.5 multiply_add_fusion
  140.0 6.8 %fusion.14 = bf16[512,1024]{1,0:T(8,128)(2,1)S(1)} fusion(bf16[512,1024]{1,0:T(8,128)(2,1)} %param.9, bf16[512,1024]{1,0:T(8,128)(2,1)} %fusion.9, bf16[2048,1024]{1,0:T(8,128)(2,1)} %all-gather.8.cloned.1.call-done, bf16[64,8,16,128]{3,2,1,0:T(8,128)(2,1)} %bitcast.70, f32[512,1024]{1,0:T(8,128)} %param.10, f32[512,1024]{1,0:T(8,128)S(1)} %copy-done.1), kind=kOutput, calls=%fused_computation.26 | convolution fusion | flops 2152726528 | bytes 13631488 | tf_op jit(solution)/shard_map/dot_general | solution.py:42
  146.8 0.3 convolution_convert_fusion.1
  147.2 0.7 reshape.168
  147.8 3.4 %all-to-all-start.1 = ((bf16[8,4,1024]{2,1,0:T(4,128)(2,1)}), bf16[8,4,1024]{2,1,0:T(4,128)(2,1)S(1)}, u32[]{:S(2)}, u32[]{:S(2)}) async-start(bf16[8,4,1024]{2,1,0:T(4,128)(2,1)} %reshape.168), calls=%async_computation.1 | async-start | bytes 131072 | tf_op jit(solution)/shard_map/all_to_all | solution.py:68
  151.2 0.3 convolution_multiply_fusion
  151.5 6.5 %all-to-all-done.1 = bf16[8,4,1024]{2,1,0:T(4,128)(2,1)S(1)} async-done(((bf16[8,4,1024]{2,1,0:T(4,128)(2,1)}), bf16[8,4,1024]{2,1,0:T(4,128)(2,1)S(1)}, u32[]{:S(2)}, u32[]{:S(2)}) %all-to-all-start.1) | async-done | bytes 65568 | tf_op jit(solution)/shard_map/all_to_all | solution.py:68
  158.0 0.6 reshape.169
  158.7 1.1 fusion.31
  159.8 0.6 gather_fusion.4
  160.5 1.4 select_convert_fusion
  161.9 3.4 %all-to-all-start.2 = ((bf16[8,4,1024]{2,1,0:T(4,128)(2,1)}), bf16[8,4,1024]{2,1,0:T(4,128)(2,1)S(1)}, u32[]{:S(2)}, u32[]{:S(2)}) async-start(bf16[8,4,1024]{2,1,0:T(4,128)(2,1)} %select_convert_fusion), calls=%async_computation.2 | async-start | bytes 131072 | tf_op jit(solution)/shard_map/all_to_all | solution.py:97
  165.3 2.7 %gather_fusion.3 = f32[512,1024]{1,0:T(8,128)} fusion(f32[48,1024]{1,0:T(8,128)S(1)} %fusion.31, s32[1024]{0:T(1024)S(1)} %pad_clamp_fusion.3), kind=kCustom, calls=%fused_computation.3 | custom fusion | bytes 4196352 | tf_op jit(solution)/shard_map/jit(_take)/gather | solution.py:103
  167.9 4.2 %all-to-all-done.2 = bf16[8,4,1024]{2,1,0:T(4,128)(2,1)S(1)} async-done(((bf16[8,4,1024]{2,1,0:T(4,128)(2,1)}), bf16[8,4,1024]{2,1,0:T(4,128)(2,1)S(1)}, u32[]{:S(2)}, u32[]{:S(2)}) %all-to-all-start.2) | async-done | bytes 65568 | tf_op jit(solution)/shard_map/all_to_all | solution.py:97
  172.1 2.7 %gather_fusion.5 = f32[512,1024]{1,0:T(8,128)} fusion(f32[32,1024]{1,0:T(8,128)S(1)} %reshape.174, s32[1024]{0:T(1024)S(1)} %pad_clamp_fusion.1), kind=kCustom, calls=%fused_computation.5 | custom fusion | bytes 4196352 | tf_op jit(solution)/shard_map/jit(_take)/gather | solution.py:104
  174.8 4.1 %subtract_select_fusion = (f32[512,1024]{1,0:T(8,128)}, f32[512,1024]{1,0:T(8,128)}) fusion(f32[512,1024]{1,0:T(8,128)S(1)} %copy-done.1, bf16[512,1024]{1,0:T(8,128)(2,1)S(1)} %fusion.14, pred[512]{0:T(512)(128)(4,1)S(1)} %copy-done.5, f32[512,1024]{1,0:T(8,128)} %gather_fusion.5, pred[512]{0:T(512)(128)(4,1)S(1)} %copy-done.6, ...), kind=kLoop, calls=%fused_computation.33 | loop fusion | flops 4194304 | bytes 11536384 | tf_op jit(solution)/shard_map/jit(_where)/select_n | solution.py:107
  (53 shorter events, 0.3 us)
Async XLA Ops:
  7.2 2.1 %copy-start.8 = (s32[4,4]{1,0:T(4,128)S(1)}, s32[4,4]{1,0:T(4,128)}, u32[]{:S(2)}) copy-start(s32[4,4]{1,0:T(4,128)} %param.13) | copy-start | bytes 196
  7.2 39.6 %all-gather.4.cloned.1.call-start = ((), (), s32[]{:S(2)}) async-start(), calls=%async_computation.3 | async-start | bytes 5242880 | tf_op jit(solution)/shard_map/all_gather | solution.py:41
  7.9 38.9 %copy-start.1 = (f32[512,1024]{1,0:T(8,128)S(1)}, f32[512,1024]{1,0:T(8,128)}, u32[]{:S(2)}) copy-start(f32[512,1024]{1,0:T(8,128)} %param.11) | copy-start | bytes 6291460
  7.9 81.4 %all-gather.6.cloned.1.call-start = ((), (), s32[]{:S(2)}) async-start(), calls=%async_computation.4 | async-start | bytes 5242880 | tf_op jit(solution)/shard_map/all_gather | solution.py:41
  46.8 42.5 %copy-start.10 = (bf16[512,1024]{1,0:T(8,128)(2,1)S(1)}, bf16[512,1024]{1,0:T(8,128)(2,1)}, u32[]{:S(2)}) copy-start(bf16[512,1024]{1,0:T(8,128)(2,1)} %param.9) | copy-start | bytes 3145732
  54.7 42.1 %copy-start.3 = (s32[512]{0:T(512)S(1)}, s32[512]{0:T(512)}, u32[]{:S(2)}) copy-start(s32[512]{0:T(512)} %param.14) | copy-start | bytes 6148
  54.7 85.3 %all-gather.8.cloned.1.call-start = ((), (), s32[]{:S(2)}) async-start(), calls=%async_computation.5 | async-start | bytes 5242880 | tf_op jit(solution)/shard_map/all_gather | solution.py:41
  96.8 0.7 copy-start
  123.4 23.4 %copy-start.4 = (pred[512]{0:T(512)(128)(4,1)}, pred[512]{0:T(512)(128)(4,1)S(1)}, u32[]{:S(2)}) copy-start(pred[512]{0:T(512)(128)(4,1)S(1)} %get-tuple-element.10) | copy-start | bytes 1540
  126.5 11.9 %all-to-all-start = ((bf16[8,1,4]{2,1,0:T(2,128)(2,1)}), bf16[8,1,4]{2,1,0:T(2,128)(2,1)S(1)}, u32[]{:S(2)}, u32[]{:S(2)}) async-start(bf16[8,1,4]{2,1,0:T(2,128)(2,1)} %all_to_all.16), calls=%async_computation | async-start | bytes 8192 | tf_op jit(solution)/shard_map/all_to_all | solution.py:75
  132.8 14.0 %copy-start.11 = (f32[48]{0:T(128)}, f32[48]{0:T(128)S(1)}, u32[]{:S(2)}) copy-start(f32[48]{0:T(128)S(1)} %iota_convert_fusion) | copy-start | bytes 580
  138.5 8.3 %copy-start.9 = (f32[32]{0:T(128)}, f32[32]{0:T(128)S(1)}, u32[]{:S(2)}) copy-start(f32[32]{0:T(128)S(1)} %reshape.172) | copy-start | bytes 388
  146.8 28.0 %copy-start.2 = (bf16[512,1024]{1,0:T(8,128)(2,1)}, bf16[512,1024]{1,0:T(8,128)(2,1)S(1)}, u32[]{:S(2)}) copy-start(bf16[512,1024]{1,0:T(8,128)(2,1)S(1)} %fusion.14) | copy-start | bytes 3145732
  147.8 10.2 %all-to-all-start.1 = ((bf16[8,4,1024]{2,1,0:T(4,128)(2,1)}), bf16[8,4,1024]{2,1,0:T(4,128)(2,1)S(1)}, u32[]{:S(2)}, u32[]{:S(2)}) async-start(bf16[8,4,1024]{2,1,0:T(4,128)(2,1)} %reshape.168), calls=%async_computation.1 | async-start | bytes 131072 | tf_op jit(solution)/shard_map/all_to_all | solution.py:68
  161.9 10.2 %all-to-all-start.2 = ((bf16[8,4,1024]{2,1,0:T(4,128)(2,1)}), bf16[8,4,1024]{2,1,0:T(4,128)(2,1)S(1)}, u32[]{:S(2)}, u32[]{:S(2)}) async-start(bf16[8,4,1024]{2,1,0:T(4,128)(2,1)} %select_convert_fusion), calls=%async_computation.2 | async-start | bytes 131072 | tf_op jit(solution)/shard_map/all_to_all | solution.py:97
  172.1 2.7 %copy-start.5 = (pred[512]{0:T(512)(128)(4,1)S(1)}, pred[512]{0:T(512)(128)(4,1)}, u32[]{:S(2)}) copy-start(pred[512]{0:T(512)(128)(4,1)} %copy-done.4) | copy-start | bytes 1540
  172.1 2.7 %copy-start.6 = (pred[512]{0:T(512)(128)(4,1)S(1)}, pred[512]{0:T(512)(128)(4,1)}, u32[]{:S(2)}) copy-start(pred[512]{0:T(512)(128)(4,1)} %get-tuple-element.7) | copy-start | bytes 1540
  172.1 2.7 %copy-start.7 = (pred[512]{0:T(512)(128)(4,1)S(1)}, pred[512]{0:T(512)(128)(4,1)}, u32[]{:S(2)}) copy-start(pred[512]{0:T(512)(128)(4,1)} %compare_and_fusion.3) | copy-start | bytes 1540
Sparse Core Ops, SparseCore 0:
  9.6 37.1 all-gather.3
  54.8 34.4 all-gather.5
  96.9 35.6 all-gather.7
where the time goes:
time: 186 us; the launch traced here: 185 us
  waiting for transfers between devices  86.7 us (47%)
  local copies, waits for them, and re-layouts  32 us (17%)
  matrix products  26.4 us (14%)
  between operations  14.1 us (8%)
  other arithmetic  13.9 us (7%)
  starting transfers between devices  12.3 us (7%)
    all_gather x3, waiting for transfers between devices, shards(): whole = lax.all_gather(iterate, 'tile', axis=0, tiled=True)  69.7 us
    dot_general x3, matrix products, shards(): drawdown = jnp.dot(expanded, whole, preferred_element_type=jnp.float32)  22.1 us
    gather x1, local copies, waits for them, and re-layouts, owner_ranks(): well_owner[sorting] * per_owner  8.39 us
    all_to_all x1, waiting for transfers between devices, shards(): lax.all_to_all(send_values.reshape(sector_count, CAP, periods), 'sector',...  6.51 us
    scatter x1, local copies, waits for them, and re-layouts, owner_ranks(): return jnp.zeros_like(well_owner).at[sorting].set(placement)  6.18 us
    all_to_all x1, waiting for transfers between devices, shards(): lax.all_to_all(send_ranks.reshape(sector_count, CAP), 'sector', split_axi...  5.63 us
    all_to_all x1, starting transfers between devices, shards(): lax.all_to_all(send_ranks.reshape(sector_count, CAP), 'sector', split_axi...  5.51 us
    sort x1, other arithmetic, owner_ranks(): sorting = jnp.argsort(well_owner, stable=True)  5.03 us
  transfers between devices with their start and end apart: 6, of which 5 were waited for; matrix products, arithmetic and copies ran while one was open for 20% of the time, Pallas kernels for 0%

commit v1 on v0

v1 whole, which is shorter than its diff:
```python
import jax
import jax.numpy as jnp
from jax import lax
from jax.experimental import pallas as pl
from jax.experimental.pallas import tpu as pltpu
from jax.sharding import PartitionSpec as P

NB = 4
INNER = 3
CAP = 4
BLK = 128


def steps_kernel(cols_ref, mixed_ref, coef_ref, out_ref, state, picked):
    row_blocks = out_ref.shape[0] // BLK
    for step in range(INNER):
        source = mixed_ref.at[0] if step == 0 else state.at[(step + 1) % 2]
        target = out_ref if step == INNER - 1 else state.at[step % 2]

        @pl.loop(0, row_blocks)
        def _(block):
            rows = pl.ds(pl.multiple_of(block * BLK, BLK), BLK)
            for n in range(NB):
                at = pl.multiple_of(cols_ref[block * NB + n] * BLK, BLK)
                picked[n * BLK : (n + 1) * BLK, :] = source[pl.ds(at, BLK), :]
            drawdown = jnp.dot(coef_ref[rows, :], picked[...], preferred_element_type=jnp.float32)
            moved = source[rows, :].astype(jnp.float32) + mixed_ref[1, rows, :].astype(jnp.float32)
            target[rows, :] = ((moved - 0.5 * drawdown) * (1.0 / 1.5)).astype(jnp.bfloat16)


def proximal_steps(columns, mixed, coefficients):
    _, rows, width = mixed.shape
    return pl.pallas_call(
        steps_kernel,
        out_shape=jax.ShapeDtypeStruct((rows, width), jnp.bfloat16),
        in_specs=[
            pl.BlockSpec(memory_space=pltpu.SMEM),
            pl.BlockSpec(memory_space=pltpu.VMEM),
            pl.BlockSpec(memory_space=pltpu.VMEM),
        ],
        out_specs=pl.BlockSpec(memory_space=pltpu.VMEM),
        scratch_shapes=[
            pltpu.VMEM((2, rows, width), jnp.bfloat16),
            pltpu.VMEM((NB * BLK, width), jnp.bfloat16),
        ],
        compiler_params=pltpu.CompilerParams(vmem_limit_bytes=40 << 20),
    )(columns, mixed, coefficients)


def slot_roles(slot_well, well_owner, sector_count, tile_count):
    wells = well_owner.shape[0]
    self_index = lax.axis_index("sector") * tile_count + lax.axis_index("tile")
    shared = slot_well >= 0
    owner = jnp.sum(
        jnp.where(slot_well[:, None] == jnp.arange(wells)[None, :], well_owner[None, :], 0), axis=1
    )
    home = shared & (owner == self_index)
    away = shared & (owner != self_index)
    bound = (owner[:, None] // tile_count == jnp.arange(sector_count)[None, :]) & away[:, None]
    slots = slot_well.shape[0]
    earlier = jnp.arange(slots)[None, :] < jnp.arange(slots)[:, None]
    before = jnp.dot(
        earlier.astype(jnp.bfloat16), bound.astype(jnp.bfloat16), preferred_element_type=jnp.float32
    )
    position = jnp.sum(jnp.where(bound, before, 0.0), axis=1).astype(jnp.int32)
    place = jnp.where(away, owner // tile_count * CAP + position, -1)
    return shared, home, place


def shards(rates, target, prior_consensus, duals, response, block_cols, slot_well, well_owner):
    slot_count, periods = rates.shape
    sector_count = lax.axis_size("sector")
    tile_count = lax.axis_size("tile")
    buffer_rows = sector_count * CAP
    pulled = (0.5 * target.astype(jnp.float32) + 0.5 * (prior_consensus - duals)).astype(jnp.bfloat16)
    mixed = lax.all_to_all(
        jnp.stack([rates, pulled]), "tile", split_axis=2, concat_axis=1, tiled=True
    )
    coefficients = lax.all_gather(response, "tile", axis=0, tiled=True)
    columns = lax.all_gather(block_cols.reshape(-1), "tile", axis=0, tiled=True)

    shared, home, place = slot_roles(slot_well, well_owner, sector_count, tile_count)
    placing = jnp.arange(buffer_rows)[:, None] == place[None, :]
    send_wells = jnp.max(jnp.where(placing, slot_well[None, :], -1), axis=1)
    got_wells = lax.all_to_all(
        send_wells.reshape(sector_count, CAP), "sector", split_axis=0, concat_axis=0, tiled=True
    ).reshape(buffer_rows)
    matching = (got_wells[:, None] == slot_well[None, :]) & home[None, :]
    weight = 2.0 + jnp.sum(matching.astype(jnp.float32), axis=0)
    placing = placing.astype(jnp.bfloat16)
    matching = matching.astype(jnp.bfloat16)

    last = proximal_steps(columns, mixed, coefficients)
    new_rates = lax.all_to_all(last, "tile", split_axis=0, concat_axis=1, tiled=True)
    rates_wide = new_rates.astype(jnp.float32)
    offered = (rates_wide + duals).astype(jnp.bfloat16)
    send_values = jnp.dot(placing, offered, preferred_element_type=jnp.float32).astype(jnp.bfloat16)
    received = lax.all_to_all(
        send_values.reshape(sector_count, CAP, periods), "sector", split_axis=0, concat_axis=0, tiled=True
    ).reshape(buffer_rows, periods)
    added = lax.dot_general(
        matching, received, (((0,), (0,)), ((), ())), preferred_element_type=jnp.float32
    )
    mean = (2.0 * offered.astype(jnp.float32) + added) / weight[:, None]
    answers = jnp.dot(matching, mean.astype(jnp.bfloat16), preferred_element_type=jnp.float32)
    returned = lax.all_to_all(
        answers.astype(jnp.bfloat16).reshape(sector_count, CAP, periods),
        "sector", split_axis=0, concat_axis=0, tiled=True,
    ).reshape(buffer_rows, periods)
    from_peer = lax.dot_general(
        placing, returned, (((0,), (0,)), ((), ())), preferred_element_type=jnp.float32
    )
    slot_mean = jnp.where(home[:, None], mean, from_peer)
    consensus = jnp.where(shared[:, None], slot_mean, rates_wide)
    new_duals = jnp.where(shared[:, None], duals + rates_wide - consensus, duals)
    return (new_rates, new_duals, consensus)


def solution(mesh):
    both = P(("sector", "tile"), None)
    return jax.shard_map(
        shards,
        mesh=mesh,
        in_specs=(both, both, both, both, both, both, P(("sector", "tile")), P()),
        out_specs=(both, both, both),
        check_vma=False,
    )
```

time: 186 us -> 137 us (0.74)
  waiting for transfers between devices: 86.7 us -> 20.7 us
  blocking collectives: 0 us -> 42.2 us
  matrix products: 26.4 us -> 5.95 us
  local copies, waits for them, and re-layouts: 32 us -> 17 us
  Pallas kernels: 0 us -> 11 us
  other arithmetic: 13.9 us -> 4.84 us
  starting transfers between devices: 12.3 us -> 19.6 us
    all_gather x3 -> x1, waiting for transfers between devices: 69.7 us -> 0.02 us  [shards(): coefficients = lax.all_gather(response, 'tile', axis=0, tiled=True)]
    unnamed x0 -> x1, blocking collectives: none -> 32.9 us
    gather x7 -> x0, local copies, waits for them, and re-layouts: 20.6 us -> none  [the longest x1 8.39 us: owner_ranks(): well_owner[sorting] * per_owner]
    dot_general x7 -> x4, matrix products: 26.1 us -> 5.64 us  [the longest x1 4.44 us: shards(): lax.dot_general(placing, returned, (((0,), (0,)), ((), ())), preferred_el...]
    pallas_call x0 -> x1, Pallas kernels: none -> 11 us  [proximal_steps(): pl.pallas_call(steps_kernel, out_shape=jax.ShapeDtypeStruct((rows, width)...]
    all_to_all x0 -> x1, blocking collectives: none -> 9.29 us  [shards(): lax.all_to_all(answers.astype(jnp.bfloat16).reshape(sector_count, CAP, pe...]
    all_to_all x1 -> x4, local copies, waits for them, and re-layouts: 0.69 us -> 7.23 us  [the longest x1 4.68 us: shards(): lax.all_to_all(jnp.stack([rates, pulled]), 'tile', split_axis=2, concat_a...]
    scatter x1 -> x0, local copies, waits for them, and re-layouts: 6.18 us -> none  [owner_ranks(): return jnp.zeros_like(well_owner).at[sorting].set(placement)]
  transfers between devices with their start and end apart: 6 -> 5, of which waited for: 5 -> 2; matrix products, arithmetic and copies ran while one was open for 20% -> 11% of each run, Pallas kernels for 0% -> 8%
where the time goes in v1:
time: 137 us; the launch traced here: 136 us
  blocking collectives  42.2 us (31%)
  waiting for transfers between devices  20.7 us (15%)
  starting transfers between devices  19.6 us (14%)
  local copies, waits for them, and re-layouts  17 us (12%)
  between operations  14.9 us (11%)
  Pallas kernels  11 us (8%)
  matrix products  5.95 us (4%)
  other arithmetic  4.84 us (4%)
    unnamed x1, blocking collectives  32.9 us
    all_to_all x1, waiting for transfers between devices, shards(): lax.all_to_all(last, 'tile', split_axis=0, concat_axis=1, tiled=True)  13.1 us
    pallas_call x1, Pallas kernels, proximal_steps(): pl.pallas_call(steps_kernel, out_shape=jax.ShapeDtypeStruct((rows, width)...  11 us
    all_to_all x1, blocking collectives, shards(): lax.all_to_all(answers.astype(jnp.bfloat16).reshape(sector_count, CAP, pe...  9.29 us
    all_to_all x1, waiting for transfers between devices, shards(): lax.all_to_all(send_values.reshape(sector_count, CAP, periods), 'sector',...  6.9 us
    all_to_all x1, starting transfers between devices, shards(): lax.all_to_all(send_values.reshape(sector_count, CAP, periods), 'sector',...  5.99 us
    all_to_all x1, starting transfers between devices, shards(): lax.all_to_all(send_wells.reshape(sector_count, CAP), 'sector', split_axi...  5.52 us
    unnamed x25, local copies, waits for them, and re-layouts  4.73 us
  transfers between devices with their start and end apart: 5, of which 2 were waited for; matrix products, arithmetic and copies ran while one was open for 11% of the time, Pallas kernels for 8%

profile of v1, /device:TPU:0, one launch (start us, length us, event | category | flops | bytes accessed | tf_op | source)
XLA Modules:
  0.0 136.1 jit_solution(17411902013910885531)
XLA Ops:
  7.2 0.0 all-gather.2.cloned.1.call-start
  7.2 0.7 all-gather.2.cloned.1.call-update
  7.9 0.0 copy-start.6
  7.9 3.2 %fusion.2 = bf16[1,512,1024]{2,1,0:T(8,128)(2,1)S(1)} fusion(f32[512,1024]{1,0:T(8,128)} %param.10, f32[512,1024]{1,0:T(8,128)} %param.11, bf16[512,1024]{1,0:T(8,128)(2,1)} %param.9), kind=kLoop, calls=%fused_computation.13 | loop fusion | flops 2621440 | bytes 6291456 | tf_op jit(solution)/shard_map/stack | solution.py:77
  11.1 0.0 copy-done.6
  11.1 0.2 pad_maximum_fusion
  11.3 4.0 %copy.26 = bf16[2,512,1024]{1,0,2:T(2,128)(2,1)} copy(bf16[2,512,1024]{2,1,0:T(8,128)(2,1)S(1)} %pad_maximum_fusion) | data formatting | bytes 4194304 | tf_op jit(solution)/shard_map/stack | solution.py:77
  15.4 4.4 %all-to-all-start = ((bf16[2,512,1024]{1,0,2:T(2,128)(2,1)}), bf16[2,512,1024]{1,0,2:T(2,128)(2,1)S(1)}, u32[]{:S(2)}, u32[]{:S(2)}) async-start(bf16[2,512,1024]{1,0,2:T(2,128)(2,1)} %copy.26), calls=%async_computation | async-start | bytes 4194304 | tf_op jit(solution)/shard_map/all_to_all | solution.py:76
  19.8 0.0 copy-done.7
  19.8 0.0 copy-done.8
  19.8 0.5 select_reduce_fusion
  20.3 0.3 fusion.1
  20.6 0.1 select_reduce_fusion.1
  20.7 0.7 all_to_all.47
  21.4 0.0 copy-done.9
  21.4 0.1 reshape.81
  21.5 0.0 copy-done.10
  21.5 0.6 dynamic-slice
  22.8 0.2 dynamic-update-slice
  23.0 32.9 %all-reduce.cols_ref = s32[64]{0:T(128)S(1)} all-reduce(s32[64]{0:T(128)S(1)} %dynamic-update-slice), channel_id=1, replica_groups=mesh['sector'=8,'tile'=4] {'tile'}, use_global_device_ids=true, to_apply=%add | all-reduce | flops 64 | bytes 512
  55.9 0.0 all-to-all-done
  55.9 5.5 %all-to-all-start.2 = ((s32[8,1,4]{2,1,0:T(1,128)}), s32[8,1,4]{2,1,0:T(1,128)S(1)}, u32[]{:S(2)}, u32[]{:S(2)}) async-start(s32[8,1,4]{2,1,0:T(1,128)} %bitcast.8), calls=%async_computation.2 | async-start | bytes 8192 | tf_op jit(solution)/shard_map/all_to_all | solution.py:85
  61.4 0.0 copy-done.3
  61.5 4.7 %copy.27 = bf16[2,512,4,256]{3,1,2,0:T(8,128)(2,1)S(1)} copy(bf16[2,512,4,256]{1,0,3,2:T(2,128)(2,1)} %bitcast.20) | data formatting | bytes 4194304 | tf_op jit(solution)/shard_map/all_to_all | solution.py:76
  66.1 0.0 all-gather.2.cloned.1.call-done.coef_ref
  66.2 0.0 copy-start
  66.2 1.6 %copy-done = bf16[2048,512]{1,0:T(8,128)(2,1)S(1)} copy-done((bf16[2048,512]{1,0:T(8,128)(2,1)S(1)}, bf16[2048,512]{1,0:T(8,128)(2,1)}, u32[]{:S(2)}) %copy-start) | copy-done | bytes 2097176
  67.8 11.0 %shard_map.103 = bf16[2048,256]{1,0:T(8,128)(2,1)} custom-call(s32[64]{0:T(128)S(1)} %all-reduce.cols_ref, bf16[2,2048,256]{2,1,0:T(8,128)(2,1)S(1)} %bitcast.15, bf16[2048,512]{1,0:T(8,128)(2,1)S(1)} %copy-done), custom_call_target="tpu_custom_call" | custom-call | tf_op jit(solution)/shard_map/pallas_call | solution.py:33
  78.8 0.0 all-to-all-done.2
  78.8 3.6 %all-to-all-start.1 = ((bf16[4,512,256]{2,1,0:T(8,128)(2,1)}), bf16[4,512,256]{2,1,0:T(8,128)(2,1)S(1)}, u32[]{:S(2)}, u32[]{:S(2)}) async-start(bf16[4,512,256]{2,1,0:T(8,128)(2,1)} %bitcast.6), calls=%async_computation.1 | async-start | bytes 2097152 | tf_op jit(solution)/shard_map/all_to_all | solution.py:94
  82.4 0.5 broadcast.63
  83.0 0.7 reduce.3
  83.6 0.1 eq.69
  83.7 0.1 convert_reduce_fusion
  83.8 13.1 %all-to-all-done.1 = bf16[4,512,256]{2,1,0:T(8,128)(2,1)S(1)} async-done(((bf16[4,512,256]{2,1,0:T(8,128)(2,1)}), bf16[4,512,256]{2,1,0:T(8,128)(2,1)S(1)}, u32[]{:S(2)}, u32[]{:S(2)}) %all-to-all-start.1) | async-done | bytes 1048608 | tf_op jit(solution)/shard_map/all_to_all | solution.py:94
  96.9 1.0 copy-done.5
  97.8 1.4 copy.30
  99.2 0.0 copy-start.2
  99.2 0.3 convolution_convert_fusion.1
  99.5 0.7 reshape.77
  100.3 6.0 %all-to-all-start.3 = ((bf16[8,4,1024]{2,1,0:T(4,128)(2,1)}), bf16[8,4,1024]{2,1,0:T(4,128)(2,1)S(1)}, u32[]{:S(2)}, u32[]{:S(2)}) async-start(bf16[8,4,1024]{2,1,0:T(4,128)(2,1)} %reshape.77), calls=%async_computation.3 | async-start | bytes 131072 | tf_op jit(solution)/shard_map/all_to_all | solution.py:98
  106.3 6.9 %all-to-all-done.3 = bf16[8,4,1024]{2,1,0:T(4,128)(2,1)S(1)} async-done(((bf16[8,4,1024]{2,1,0:T(4,128)(2,1)}), bf16[8,4,1024]{2,1,0:T(4,128)(2,1)S(1)}, u32[]{:S(2)}, u32[]{:S(2)}) %all-to-all-start.3) | async-done | bytes 65568 | tf_op jit(solution)/shard_map/all_to_all | solution.py:98
  113.2 0.6 add_divide_fusion
  113.8 0.0 copy-start.4
  113.8 1.3 copy-done.4
  115.2 0.3 convolution_convert_fusion
  115.5 9.3 %all_to_all.56 = bf16[8,4,1024]{2,1,0:T(4,128)(2,1)S(1)} all-to-all(bf16[8,4,1024]{2,1,0:T(4,128)(2,1)S(1)} %reshape.79), channel_id=1, replica_groups=mesh['sector'=8,'tile'=4] {'sector'}, dimensions={0} | all-to-all | bytes 131072 | tf_op jit(solution)/shard_map/all_to_all | solution.py:106
  124.8 4.4 %subtract_select_fusion = (f32[512,1024]{1,0:T(8,128)}, f32[512,1024]{1,0:T(8,128)}) fusion(f32[512,1024]{1,0:T(8,128)S(1)} %copy-done.1, bf16[512,1024]{1,0:T(8,128)(2,1)S(1)} %bitcast.18, pred[512]{0:T(512)(128)(4,1)S(1)} %get-tuple-element.4, f32[512,1024]{1,0:T(8,128)} %copy-done.4, bf16[32,1024]{1,0:T(8,128)(2,1)S(1)} %reshape.80, ...), kind=kOutput, calls=%fused_computation.5 | convolution fusion | flops 36716544 | bytes 9505792 | tf_op jit(solution)/shard_map/dot_general | solution.py:110
  (18 shorter events, 0.1 us)
Async XLA Ops:
  7.2 59.0 %all-gather.2.cloned.1.call-start = ((), (), s32[]{:S(2)}) async-start(), calls=%async_computation.5 | async-start | bytes 2621440 | tf_op jit(solution)/shard_map/all_gather | solution.py:79
  7.9 3.2 %copy-start.6 = (bf16[512,1024]{1,0:T(8,128)(2,1)S(1)}, bf16[512,1024]{1,0:T(8,128)(2,1)}, u32[]{:S(2)}) copy-start(bf16[512,1024]{1,0:T(8,128)(2,1)} %param.8) | copy-start | bytes 3145732
  15.4 4.4 %copy-start.7 = (s32[512]{0:T(512)S(1)}, s32[512]{0:T(512)}, u32[]{:S(2)}) copy-start(s32[512]{0:T(512)} %param.14) | copy-start | bytes 6148
  15.4 4.4 %copy-start.8 = (s32[1536]{0:T(1024)S(1)}, s32[1536]{0:T(1024)}, u32[]{:S(2)}) copy-start(s32[1536]{0:T(1024)} %param.15) | copy-start | bytes 18436
  15.4 6.1 %copy-start.9 = (s32[4,4]{1,0:T(4,128)S(1)}, s32[4,4]{1,0:T(4,128)}, u32[]{:S(2)}) copy-start(s32[4,4]{1,0:T(4,128)} %param.13) | copy-start | bytes 196
  15.4 6.1 %copy-start.10 = (u32[32]{0:T(128)S(1)}, u32[32]{0:T(128)}, u32[]{:S(2)}) copy-start(u32[32]{0:T(128)} %constant.51) | copy-start | bytes 388
  15.4 40.5 %all-to-all-start = ((bf16[2,512,1024]{1,0,2:T(2,128)(2,1)}), bf16[2,512,1024]{1,0,2:T(2,128)(2,1)S(1)}, u32[]{:S(2)}, u32[]{:S(2)}) async-start(bf16[2,512,1024]{1,0,2:T(2,128)(2,1)} %copy.26), calls=%async_computation | async-start | bytes 4194304 | tf_op jit(solution)/shard_map/all_to_all | solution.py:76
  55.9 5.5 %copy-start.3 = (bf16[2,512,1024]{1,0,2:T(2,128)(2,1)}, bf16[2,512,1024]{1,0,2:T(2,128)(2,1)S(1)}, u32[]{:S(2)}) copy-start(bf16[2,512,1024]{1,0,2:T(2,128)(2,1)S(1)} %all-to-all-done) | copy-start | bytes 6291460
  55.9 22.9 %all-to-all-start.2 = ((s32[8,1,4]{2,1,0:T(1,128)}), s32[8,1,4]{2,1,0:T(1,128)S(1)}, u32[]{:S(2)}, u32[]{:S(2)}) async-start(s32[8,1,4]{2,1,0:T(1,128)} %bitcast.8), calls=%async_computation.2 | async-start | bytes 8192 | tf_op jit(solution)/shard_map/all_to_all | solution.py:85
  66.2 1.6 %copy-start = (bf16[2048,512]{1,0:T(8,128)(2,1)S(1)}, bf16[2048,512]{1,0:T(8,128)(2,1)}, u32[]{:S(2)}) copy-start(bf16[2048,512]{1,0:T(8,128)(2,1)} %all-gather.2.cloned.1.call-done.coef_ref) | copy-start | bytes 6291460
  78.8 20.4 %copy-start.1 = (f32[512,1024]{1,0:T(8,128)S(1)}, f32[512,1024]{1,0:T(8,128)}, u32[]{:S(2)}) copy-start(f32[512,1024]{1,0:T(8,128)} %param.11) | copy-start | bytes 6291460
  78.8 18.1 %all-to-all-start.1 = ((bf16[4,512,256]{2,1,0:T(8,128)(2,1)}), bf16[4,512,256]{2,1,0:T(8,128)(2,1)S(1)}, u32[]{:S(2)}, u32[]{:S(2)}) async-start(bf16[4,512,256]{2,1,0:T(8,128)(2,1)} %bitcast.6), calls=%async_computation.1 | async-start | bytes 2097152 | tf_op jit(solution)/shard_map/all_to_all | solution.py:94
  96.9 1.0 copy-start.5
  99.2 25.6 %copy-start.2 = (bf16[4,64,8,256]{3,2,0,1:T(8,128)(2,1)}, bf16[4,64,8,256]{3,2,0,1:T(8,128)(2,1)S(1)}, u32[]{:S(2)}) copy-start(bf16[4,64,8,256]{3,2,0,1:T(8,128)(2,1)S(1)} %copy.30) | copy-start | bytes 3145732
  100.3 12.9 %all-to-all-start.3 = ((bf16[8,4,1024]{2,1,0:T(4,128)(2,1)}), bf16[8,4,1024]{2,1,0:T(4,128)(2,1)S(1)}, u32[]{:S(2)}, u32[]{:S(2)}) async-start(bf16[8,4,1024]{2,1,0:T(4,128)(2,1)} %reshape.77), calls=%async_computation.3 | async-start | bytes 131072 | tf_op jit(solution)/shard_map/all_to_all | solution.py:98
  113.8 1.3 copy-start.4
Sparse Core Ops, SparseCore 0:
  9.6 35.8 all-gather.1

commit v2 on v1

v2 whole, which is shorter than its diff:
```python
import functools

import jax
import jax.numpy as jnp
from jax import lax
from jax.experimental import pallas as pl
from jax.experimental.pallas import tpu as pltpu
from jax.sharding import PartitionSpec as P

NB = 4
INNER = 3
CAP = 4
BLK = 128
TILES = 4
SLAB = CAP * TILES
MESH = pl.DeviceIdType.MESH


def round_kernel(
    sectors,
    rates, target, prior, duals, response, cols, roles, role_cols,
    new_rates, new_duals, consensus,
    start, pull, pull_out, coef, state, last, got_rates, drawn, dense,
    cols_all, target_v, prior_v, duals_v, placing, matching,
    wells_out, wells_in, offered, values_out, values_in, answers_out, answers_in, mean, duals_o, cons_o,
    local_sem, tile_send, tile_recv, sector_send, sector_recv, out_sem,
):
    slots, periods = rates.shape
    width = periods // TILES
    own = lax.axis_index("tile")
    sector = lax.axis_index("sector")
    peer = [own, own + 1 - 2 * (own % 2), (own + 2) % TILES, TILES - 1 - own]

    def slot_rows(tile):
        return pl.ds(pl.multiple_of(tile * slots, slots), slots)

    def share(tile):
        return pl.ds(pl.multiple_of(tile * width, width), width)

    def to_tile(phase, k, source, dest, via=None):
        return pltpu.make_async_remote_copy(
            src_ref=source, dst_ref=dest,
            send_sem=tile_send.at[phase, k], recv_sem=tile_recv.at[phase, k],
            device_id={"tile": peer[k if via is None else via]}, device_id_type=MESH,
        )

    def to_sector(phase, j, source, dest):
        return pltpu.make_async_remote_copy(
            src_ref=source, dst_ref=dest,
            send_sem=sector_send.at[phase, j], recv_sem=sector_recv.at[phase, j],
            device_id={"sector": lax.rem(sector + j, sectors)}, device_id_type=MESH,
        )

    def slab(index):
        return pl.ds(pl.multiple_of(index * SLAB, SLAB), SLAB)

    barrier = pltpu.get_barrier_semaphore()
    for k in range(1, TILES):
        pl.semaphore_signal(barrier, inc=1, device_id={"tile": peer[k]}, device_id_type=MESH)

    @pl.loop(1, sectors)
    def _(j):
        pl.semaphore_signal(
            barrier, inc=1, device_id={"sector": lax.rem(sector + j, sectors)}, device_id_type=MESH
        )

    loads = [
        pltpu.make_async_copy(a, b, local_sem.at[i])
        for i, (a, b) in enumerate([
            (target, target_v), (prior, prior_v), (duals, duals_v),
            (rates.at[:, share(own)], start.at[slot_rows(own), :]),
            (response, coef.at[slot_rows(own), :]),
        ])
    ]
    for copy in loads:
        copy.start()
    col_count = cols.shape[0]

    def col_rows_of(tile):
        return pl.ds(pl.multiple_of(tile * col_count, col_count), col_count)

    col_rows = col_rows_of(own)
    cols_all[col_rows, :] = cols[...]
    pl.semaphore_wait(barrier, TILES - 1 + sectors - 1)

    sends = []

    def send(phase, k, source, dest, via=None):
        copy = to_tile(phase, k, source, dest, via)
        copy.start()
        sends.append(copy)

    for k in (2, 3, 1):
        send(0, k, cols, cols_all.at[col_rows, :])
    send(1, 2, response, coef.at[slot_rows(own), :])
    for k in (2, 3):
        send(2, k, rates.at[:, share(peer[k])], start.at[slot_rows(own), :])
    send(1, 1, response, coef.at[slot_rows(own), :])
    send(2, 1, rates.at[:, share(peer[1])], start.at[slot_rows(own), :])

    for copy in loads[:3]:
        copy.wait()

    def pull_of(k):
        at = share(peer[k])
        value = 0.5 * target_v[:, at].astype(jnp.float32) + 0.5 * (prior_v[:, at] - duals_v[:, at])
        return value.astype(jnp.bfloat16)

    for k in (2, 3, 1):
        pull_out[k] = pull_of(k)
        send(3, k, pull_out.at[k], pull.at[slot_rows(own), :])
    pull[slot_rows(own), :] = pull_of(0)

    place_row, well_row, home_row = roles[0:1, :], roles[1:2, :], roles[2:3, :] > 0
    row = lax.broadcasted_iota(jnp.int32, (sectors * SLAB, 1), 0)
    chunk = (row % SLAB) // CAP
    placed = place_row == (row // SLAB) * CAP + row % CAP
    wells = jnp.max(jnp.where(placed, well_row, -1), axis=1, keepdims=True)
    wells_out[...] = jnp.broadcast_to(wells, wells_out.shape)
    for q in range(TILES):
        placing[q] = jnp.where(placed & (chunk == q), 1.0, 0.0).astype(jnp.bfloat16)
    wells_in[slab(sector), :] = jnp.full((SLAB, 128), -1, jnp.int32)
    values_in[slab(sector), :] = jnp.zeros((SLAB, width), jnp.bfloat16)
    answers_in[slab(sector), :] = jnp.zeros((SLAB, width), jnp.bfloat16)

    def exchange(phase, source, dest):
        @pl.loop(1, sectors)
        def _(j):
            to_sector(
                phase, j, source.at[slab(lax.rem(sector + j, sectors)), :], dest.at[slab(sector), :]
            ).start()

    def arrived(phase, source, dest):
        @pl.loop(1, sectors)
        def _(j):
            to_sector(
                phase, j, source.at[slab(lax.rem(sector + j, sectors)), :],
                dest.at[slab(lax.rem(sector + sectors - j, sectors)), :],
            ).wait()

    exchange(0, wells_out, wells_in)

    def recv(phase, k, ref):
        to_tile(phase, k, ref, ref).wait_recv()

    per_tile = slots // BLK

    def expand(tile):
        names = cols_all[col_rows_of(tile), :]
        for inner in range(per_tile):
            rows = pl.ds(pl.multiple_of(tile * slots + inner * BLK, BLK), BLK)
            blocks = [coef[rows, n * BLK : (n + 1) * BLK].astype(jnp.float32) for n in range(NB)]
            for c in range(per_tile * TILES):
                value = jnp.zeros((BLK, BLK), jnp.float32)
                for n in range(NB):
                    name = names[inner * NB + n : inner * NB + n + 1, :]
                    value = jnp.where(name == c, blocks[n], value)
                dense[rows, c * BLK : (c + 1) * BLK] = value.astype(jnp.bfloat16)

    recv(1, 2, coef.at[slot_rows(peer[2]), :])
    send(1, 3, coef.at[slot_rows(peer[2]), :], coef.at[slot_rows(peer[2]), :], 1)
    arrived(0, wells_out, wells_in)
    match = (wells_in[:, 0:1] == well_row) & home_row
    for q in range(TILES):
        matching[q] = jnp.where(match & (chunk == q), 1.0, 0.0).astype(jnp.bfloat16)
    heard = lax.dot_general(
        matching[0], jnp.ones((sectors * SLAB, 128), jnp.bfloat16),
        (((0,), (0,)), ((), ())), preferred_element_type=jnp.float32,
    )
    scale = 1.0 / (2.0 + heard[:, 0:1])

    for copy in loads[3:]:
        copy.wait()
    for k in (1, 2, 3):
        recv(0, k, cols_all.at[col_rows_of(peer[k]), :])
    expand(own)
    recv(1, 1, coef.at[slot_rows(peer[1]), :])
    expand(peer[1])
    expand(peer[2])
    recv(1, 3, coef.at[slot_rows(peer[3]), :])
    expand(peer[3])
    for k in (1, 2, 3):
        recv(2, k, start.at[slot_rows(peer[k]), :])

    part = 256

    def drawdown(at, source):
        rows = pl.ds(pl.multiple_of(at, part), part)
        return rows, jnp.dot(dense[rows, :], source[...], preferred_element_type=jnp.float32)

    def stepped(rows, source, drawn_rows):
        moved = source[rows, :].astype(jnp.float32) + pull[rows, :].astype(jnp.float32)
        return ((moved - 0.5 * drawn_rows) * (1.0 / 1.5)).astype(jnp.bfloat16)

    @pl.loop(0, slots * TILES // part)
    def _(block):
        rows, value = drawdown(block * part, start)
        drawn[rows, :] = value

    for k in (1, 2, 3):
        recv(3, k, pull.at[slot_rows(peer[k]), :])

    @pl.loop(0, per_tile * TILES)
    def _(block):
        rows = pl.ds(pl.multiple_of(block * BLK, BLK), BLK)
        state[0, rows, :] = stepped(rows, start, drawn[rows, :])

    for step in range(1, INNER - 1):
        source = state.at[(step + 1) % 2]
        dest = state.at[step % 2]

        @pl.loop(0, slots * TILES // part)
        def _(block):
            rows, value = drawdown(block * part, source)
            dest[rows, :] = stepped(rows, source, value)

    source = state.at[INNER % 2]
    for k in (2, 3, 1, 0):
        for inner in range(slots // part):
            rows, value = drawdown(peer[k] * slots + inner * part, source)
            result = stepped(rows, source, value)
            if k == 0:
                got_rates[own, inner * part : (inner + 1) * part, :] = result
            else:
                last[k, inner * part : (inner + 1) * part, :] = result
        if k > 0:
            send(4, k, last.at[k], got_rates.at[own])

    outs = []

    def put(i, source, dest):
        copy = pltpu.make_async_copy(source, dest, out_sem.at[i])
        copy.start()
        outs.append(copy)

    total = jnp.zeros((sectors * SLAB, width), jnp.float32)
    for k in range(TILES):
        q = peer[k]
        if k > 0:
            recv(4, k, got_rates.at[q])
        put(k, got_rates.at[q], new_rates.at[:, share(q)])
        offer = (got_rates[q].astype(jnp.float32) + duals_v[:, share(q)]).astype(jnp.bfloat16)
        offered[k] = offer
        total += jnp.dot(placing[q], offer, preferred_element_type=jnp.float32)
    values_out[...] = total.astype(jnp.bfloat16)
    exchange(1, values_out, values_in)
    arrived(1, values_out, values_in)
    total = jnp.zeros((sectors * SLAB, width), jnp.float32)
    for k in range(TILES):
        q = peer[k]
        added = lax.dot_general(
            matching[q], values_in[...], (((0,), (0,)), ((), ())), preferred_element_type=jnp.float32
        )
        value = (2.0 * offered[k].astype(jnp.float32) + added) * scale
        mean[k] = value
        total += jnp.dot(matching[q], value.astype(jnp.bfloat16), preferred_element_type=jnp.float32)
    answers_out[...] = total.astype(jnp.bfloat16)
    exchange(2, answers_out, answers_in)
    home, shared = role_cols[:, 0:1] > 0, role_cols[:, 1:2] > 0
    arrived(2, answers_out, answers_in)
    for k in range(TILES):
        q = peer[k]
        from_peer = lax.dot_general(
            placing[q], answers_in[...], (((0,), (0,)), ((), ())), preferred_element_type=jnp.float32
        )
        wide = got_rates[q].astype(jnp.float32)
        agreed = jnp.where(home, mean[k], jnp.where(shared, from_peer, wide))
        cons_o[k] = agreed
        put(4 + k, cons_o.at[k], consensus.at[:, share(q)])
        kept = duals_v[:, share(q)]
        duals_o[k] = jnp.where(shared, kept + wide - agreed, kept)
        put(8 + k, duals_o.at[k], new_duals.at[:, share(q)])
    for copy in outs:
        copy.wait()
    for copy in sends:
        copy.wait_send()


def slot_roles(slot_well, well_owner, sector_count, tile_count):
    wells = well_owner.shape[0]
    self_index = lax.axis_index("sector") * tile_count + lax.axis_index("tile")
    shared = slot_well >= 0
    owner = jnp.sum(
        jnp.where(slot_well[:, None] == jnp.arange(wells)[None, :], well_owner[None, :], 0), axis=1
    )
    home = shared & (owner == self_index)
    away = shared & (owner != self_index)
    bound = (owner[:, None] // tile_count == jnp.arange(sector_count)[None, :]) & away[:, None]
    slots = slot_well.shape[0]
    earlier = jnp.arange(slots)[None, :] < jnp.arange(slots)[:, None]
    before = jnp.dot(
        earlier.astype(jnp.bfloat16), bound.astype(jnp.bfloat16), preferred_element_type=jnp.float32
    )
    position = jnp.sum(jnp.where(bound, before, 0.0), axis=1).astype(jnp.int32)
    place = jnp.where(away, owner // tile_count * CAP + position, -1)
    return shared, home, place


def shards(rates, target, prior_consensus, duals, response, block_cols, slot_well, well_owner):
    slots, periods = rates.shape
    sectors = lax.axis_size("sector")
    width = periods // TILES
    rows = TILES * slots
    slabs = sectors * SLAB
    shared, home, place = slot_roles(slot_well, well_owner, sectors, TILES)
    shared, home = shared.astype(jnp.int32), home.astype(jnp.int32)
    empty = jnp.zeros_like(place)
    roles = jnp.stack([place, slot_well, home] + [empty] * 5)
    role_cols = jnp.stack([home, shared], axis=1)
    cols = jnp.broadcast_to(block_cols.reshape(-1, 1), (block_cols.size, 128))
    bf16, f32, i32 = jnp.bfloat16, jnp.float32, jnp.int32
    whole = pl.BlockSpec(memory_space=pltpu.VMEM)
    far = pl.BlockSpec(memory_space=pl.ANY)
    dma = pltpu.SemaphoreType.DMA
    return pl.pallas_call(
        functools.partial(round_kernel, sectors),
        out_shape=(
            jax.ShapeDtypeStruct((slots, periods), bf16),
            jax.ShapeDtypeStruct((slots, periods), f32),
            jax.ShapeDtypeStruct((slots, periods), f32),
        ),
        in_specs=[far] * 5 + [whole] * 3,
        out_specs=(far, far, far),
        scratch_shapes=[
            pltpu.VMEM((rows, width), bf16),
            pltpu.VMEM((rows, width), bf16),
            pltpu.VMEM((TILES, slots, width), bf16),
            pltpu.VMEM((rows, NB * BLK), bf16),
            pltpu.VMEM((2, rows, width), bf16),
            pltpu.VMEM((TILES, slots, width), bf16),
            pltpu.VMEM((TILES, slots, width), bf16),
            pltpu.VMEM((rows, width), f32),
            pltpu.VMEM((rows, rows), bf16),
            pltpu.VMEM((TILES * block_cols.size, 128), i32),
            pltpu.VMEM((slots, periods), bf16),
            pltpu.VMEM((slots, periods), f32),
            pltpu.VMEM((slots, periods), f32),
            pltpu.VMEM((TILES, slabs, slots), bf16),
            pltpu.VMEM((TILES, slabs, slots), bf16),
            pltpu.VMEM((slabs, 128), i32),
            pltpu.VMEM((slabs, 128), i32),
            pltpu.VMEM((TILES, slots, width), bf16),
            pltpu.VMEM((slabs, width), bf16),
            pltpu.VMEM((slabs, width), bf16),
            pltpu.VMEM((slabs, width), bf16),
            pltpu.VMEM((slabs, width), bf16),
            pltpu.VMEM((TILES, slots, width), f32),
            pltpu.VMEM((TILES, slots, width), f32),
            pltpu.VMEM((TILES, slots, width), f32),
            dma((5,)),
            dma((5, TILES)),
            dma((5, TILES)),
            dma((3, sectors)),
            dma((3, sectors)),
            dma((12,)),
        ],
        compiler_params=pltpu.CompilerParams(
            collective_id=0, has_side_effects=True, vmem_limit_bytes=56 << 20
        ),
    )(rates, target, prior_consensus, duals, response, cols, roles, role_cols)


def solution(mesh):
    both = P(("sector", "tile"), None)
    return jax.shard_map(
        shards,
        mesh=mesh,
        in_specs=(both, both, both, both, both, both, P(("sector", "tile")), P()),
        out_specs=(both, both, both),
        check_vma=False,
    )
```

time: 137 us -> 86.2 us (0.63)
  Pallas kernels: 11 us -> 73.3 us
  blocking collectives: 42.2 us -> 0 us
  waiting for transfers between devices: 20.7 us -> 0 us
  starting transfers between devices: 19.6 us -> 0 us
  between operations: 14.9 us -> 0.68 us
  local copies, waits for them, and re-layouts: 17 us -> 9.68 us
  matrix products: 5.95 us -> 0.26 us
  other arithmetic: 4.84 us -> 1.98 us
    pallas_call x1, Pallas kernels: 11 us -> 73.3 us  [shards(): pl.pallas_call(functools.partial(round_kernel, sectors), out_shape=(jax.S...]
    unnamed x1 -> x0, blocking collectives: 32.9 us -> none
    all_to_all x4 -> x0, waiting for transfers between devices: 20 us -> none  [the longest x1 13.1 us: shards(): lax.all_to_all(last, 'tile', split_axis=0, concat_axis=1, tiled=True)]
    all_to_all x4 -> x0, starting transfers between devices: 19.5 us -> none  [the longest x1 5.99 us: shards(): lax.all_to_all(send_values.reshape(sector_count, CAP, periods), 'sector',...]
    all_to_all x1 -> x0, blocking collectives: 9.29 us -> none  [shards(): lax.all_to_all(answers.astype(jnp.bfloat16).reshape(sector_count, CAP, pe...]
    all_to_all x4 -> x0, local copies, waits for them, and re-layouts: 7.23 us -> none  [the longest x1 4.68 us: shards(): lax.all_to_all(jnp.stack([rates, pulled]), 'tile', split_axis=2, concat_a...]
    dot_general x4 -> x0, matrix products: 5.69 us -> none  [the longest x1 4.44 us: shards(): lax.dot_general(placing, returned, (((0,), (0,)), ((), ())), preferred_el...]
    another operation x2, other arithmetic: 3.38 us -> 0.7 us  [shards(): role_cols = jnp.stack([home, shared], axis=1)]
  transfers between devices with their start and end apart: 5 -> 0, of which waited for: 2 -> 0; matrix products, arithmetic and copies ran while one was open for 11% -> 0% of each run, Pallas kernels for 8% -> 0%
where the time goes in v2:
time: 86.2 us; the launch traced here: 85.9 us
  Pallas kernels  73.3 us (85%)
  local copies, waits for them, and re-layouts  9.68 us (11%)
  other arithmetic  1.98 us (2%)
    pallas_call x1, Pallas kernels, shards(): pl.pallas_call(functools.partial(round_kernel, sectors), out_shape=(jax.S...  73.3 us
    unnamed x7, local copies, waits for them, and re-layouts  6.08 us

profile of v2, /device:TPU:0, one launch (start us, length us, event | category | flops | bytes accessed | tf_op | source)
XLA Modules:
  0.0 85.9 jit_solution(15779968496289420047)
XLA Ops:
  0.6 0.8 broadcast_in_dim.22
  1.4 1.2 %select_reduce_fusion = s32[512]{0:T(512)S(1)} fusion(s32[1536]{0:T(1024)} %param.15, s32[512]{0:T(512)} %param.14), kind=kLoop, calls=%fused_computation | loop fusion | flops 2358784 | bytes 10240 | tf_op jit(solution)/shard_map/reduce_sum | solution.py:283
  2.7 0.7 fusion.7
  3.4 0.3 fusion
  3.7 0.7 broadcast_in_dim.34.cols
  4.3 1.3 %stack.31.roles = s32[8,512]{1,0:T(8,128)} concatenate(s32[1,512]{1,0:T(1,128)S(1)} %bitcast.8, s32[1,512]{1,0:T(1,128)} %bitcast.5, s32[1,512]{1,0:T(1,128)S(1)} %bitcast.7, s32[1,512]{1,0:T(1,128)S(1)} %stack_broadcast_in_dim.3, s32[4,512]{1,0:T(4,128)S(1)} %stack.30), dimensions={0} | concatenate | bytes 32768 | tf_op jit(solution)/shard_map/stack | solution.py:308
  5.6 0.9 copy.14.role_cols
  6.5 73.3 %shard_map.103 = (bf16[512,1024]{1,0:T(8,128)(2,1)}, f32[512,1024]{1,0:T(8,128)}, f32[512,1024]{1,0:T(8,128)}) custom-call(bf16[512,1024]{1,0:T(8,128)(2,1)} %rates.1, bf16[512,1024]{1,0:T(8,128)(2,1)} %target.1, f32[512,1024]{1,0:T(8,128)} %prior.1, f32[512,1024]{1,0:T(8,128)} %duals.1, bf16[512,512]{1,0:T(8,128)(2,1)} %response.1, ...), custom_call_target="tpu_custom_call" | custom-call | tf_op jit(solution)/shard_map/pallas_call | solution.py:315
  79.8 0.0 copy-start.1
  79.8 2.4 %copy.18 = bf16[512,1024]{1,0:T(8,128)(2,1)} copy(bf16[512,1024]{1,0:T(8,128)(2,1)} %get-tuple-element.10) | data formatting | bytes 2097152
  82.2 0.0 copy-done.1
  82.2 0.0 copy-start
  82.2 1.3 %copy.19 = f32[512,1024]{1,0:T(8,128)} copy(f32[512,1024]{1,0:T(8,128)S(1)} %copy-done.1) | data formatting | bytes 4194304
  83.6 1.0 %copy-done = f32[512,1024]{1,0:T(8,128)S(1)} copy-done((f32[512,1024]{1,0:T(8,128)S(1)}, f32[512,1024]{1,0:T(8,128)}, u32[]{:S(2)}) %copy-start) | copy-done | bytes 2097176
  84.6 1.3 %copy.20 = f32[512,1024]{1,0:T(8,128)} copy(f32[512,1024]{1,0:T(8,128)S(1)} %copy-done) | data formatting | bytes 4194304
  (6 shorter events, 0.0 us)
Async XLA Ops:
  79.8 2.4 %copy-start.1 = (f32[512,1024]{1,0:T(8,128)S(1)}, f32[512,1024]{1,0:T(8,128)}, u32[]{:S(2)}) copy-start(f32[512,1024]{1,0:T(8,128)} %get-tuple-element.11) | copy-start | bytes 6291460
  82.2 2.3 %copy-start = (f32[512,1024]{1,0:T(8,128)S(1)}, f32[512,1024]{1,0:T(8,128)}, u32[]{:S(2)}) copy-start(f32[512,1024]{1,0:T(8,128)} %get-tuple-element.12) | copy-start | bytes 6291460

commit v3 on v2

--- a/solution.py
+++ b/solution.py
@@ -18,11 +18,11 @@
 
 def round_kernel(
     sectors,
-    rates, target, prior, duals, response, cols, roles, role_cols,
-    new_rates, new_duals, consensus,
+    rates, target, prior, duals, response, cols, slot_well, well_owner,
+    rates_o, placing_o, matching_o, values_o, answers_o, roles_o,
     start, pull, pull_out, coef, state, last, got_rates, drawn, dense,
     cols_all, target_v, prior_v, duals_v, placing, matching,
-    wells_out, wells_in, offered, values_out, values_in, answers_out, answers_in, mean, duals_o, cons_o,
+    wells_out, wells_in, offered, values_out, values_in, answers_out, answers_in, roles_v,
     local_sem, tile_send, tile_recv, sector_send, sector_recv, out_sem,
 ):
     slots, periods = rates.shape
@@ -111,7 +111,37 @@
         send(3, k, pull_out.at[k], pull.at[slot_rows(own), :])
     pull[slot_rows(own), :] = pull_of(0)
 
-    place_row, well_row, home_row = roles[0:1, :], roles[1:2, :], roles[2:3, :] > 0
+    well_row = slot_well[...]
+    group = 512
+
+    def looked_up(i, found):
+        at = pl.multiple_of(i * group, group)
+        name = lax.broadcasted_iota(jnp.int32, (group, 1), 0) + at
+        hit = jnp.where(name == well_row, 1.0, 0.0).astype(jnp.bfloat16)
+        owners = jnp.broadcast_to(well_owner[:, pl.ds(at, group)].astype(jnp.float32), (8, group))
+        return found + jnp.dot(
+            owners.astype(jnp.bfloat16), hit, preferred_element_type=jnp.float32
+        )
+
+    owner = lax.fori_loop(
+        0, well_owner.shape[1] // group, looked_up, jnp.zeros((8, slots), jnp.float32)
+    )[0:1, :].astype(jnp.int32)
+    shared_row = well_row >= 0
+    home_row = shared_row & (owner == sector * TILES + own)
+    away_row = shared_row & (owner != sector * TILES + own)
+    facing = owner // TILES
+    bound = jnp.where(
+        (lax.broadcasted_iota(jnp.int32, (sectors, 1), 0) == facing) & away_row, 1.0, 0.0
+    )
+    earlier = jnp.where(
+        lax.broadcasted_iota(jnp.int32, (slots, 1), 0) < lax.broadcasted_iota(jnp.int32, (1, slots), 1),
+        1.0, 0.0,
+    )
+    before = jnp.dot(
+        bound.astype(jnp.bfloat16), earlier.astype(jnp.bfloat16), preferred_element_type=jnp.float32
+    )
+    position = jnp.sum(bound * before, axis=0, keepdims=True).astype(jnp.int32)
+    place_row = jnp.where(away_row, facing * CAP + position, -1)
     row = lax.broadcasted_iota(jnp.int32, (sectors * SLAB, 1), 0)
     chunk = (row % SLAB) // CAP
     placed = place_row == (row // SLAB) * CAP + row % CAP
@@ -167,7 +197,21 @@
         matching[0], jnp.ones((sectors * SLAB, 128), jnp.bfloat16),
         (((0,), (0,)), ((), ())), preferred_element_type=jnp.float32,
     )
-    scale = 1.0 / (2.0 + heard[:, 0:1])
+    scale = 1.0 / (2.0 + heard)
+    roles_v[0] = scale
+    kind = jnp.where(home_row, 2.0, jnp.where(shared_row, 1.0, 0.0))
+    roles_v[1] = jnp.broadcast_to(kind, (128, slots)).T
+    scale = scale[:, 0:1]
+    outs = []
+
+    def put(i, source, dest):
+        copy = pltpu.make_async_copy(source, dest, out_sem.at[i])
+        copy.start()
+        outs.append(copy)
+
+    put(4, placing, placing_o)
+    put(5, matching, matching_o)
+    put(6, roles_v, roles_o)
 
     for copy in loads[3:]:
         copy.wait()
@@ -226,25 +270,19 @@
         if k > 0:
             send(4, k, last.at[k], got_rates.at[own])
 
-    outs = []
-
-    def put(i, source, dest):
-        copy = pltpu.make_async_copy(source, dest, out_sem.at[i])
-        copy.start()
-        outs.append(copy)
-
     total = jnp.zeros((sectors * SLAB, width), jnp.float32)
     for k in range(TILES):
         q = peer[k]
         if k > 0:
             recv(4, k, got_rates.at[q])
-        put(k, got_rates.at[q], new_rates.at[:, share(q)])
+        put(k, got_rates.at[q], rates_o.at[q])
         offer = (got_rates[q].astype(jnp.float32) + duals_v[:, share(q)]).astype(jnp.bfloat16)
         offered[k] = offer
         total += jnp.dot(placing[q], offer, preferred_element_type=jnp.float32)
     values_out[...] = total.astype(jnp.bfloat16)
     exchange(1, values_out, values_in)
     arrived(1, values_out, values_in)
+    put(7, values_in, values_o)
     total = jnp.zeros((sectors * SLAB, width), jnp.float32)
     for k in range(TILES):
         q = peer[k]
@@ -252,48 +290,31 @@
             matching[q], values_in[...], (((0,), (0,)), ((), ())), preferred_element_type=jnp.float32
         )
         value = (2.0 * offered[k].astype(jnp.float32) + added) * scale
-        mean[k] = value
         total += jnp.dot(matching[q], value.astype(jnp.bfloat16), preferred_element_type=jnp.float32)
     answers_out[...] = total.astype(jnp.bfloat16)
     exchange(2, answers_out, answers_in)
-    home, shared = role_cols[:, 0:1] > 0, role_cols[:, 1:2] > 0
     arrived(2, answers_out, answers_in)
-    for k in range(TILES):
-        q = peer[k]
-        from_peer = lax.dot_general(
-            placing[q], answers_in[...], (((0,), (0,)), ((), ())), preferred_element_type=jnp.float32
-        )
-        wide = got_rates[q].astype(jnp.float32)
-        agreed = jnp.where(home, mean[k], jnp.where(shared, from_peer, wide))
-        cons_o[k] = agreed
-        put(4 + k, cons_o.at[k], consensus.at[:, share(q)])
-        kept = duals_v[:, share(q)]
-        duals_o[k] = jnp.where(shared, kept + wide - agreed, kept)
-        put(8 + k, duals_o.at[k], new_duals.at[:, share(q)])
+    put(8, answers_in, answers_o)
     for copy in outs:
         copy.wait()
     for copy in sends:
         copy.wait_send()
 
 
-def slot_roles(slot_well, well_owner, sector_count, tile_count):
-    wells = well_owner.shape[0]
-    self_index = lax.axis_index("sector") * tile_count + lax.axis_index("tile")
-    shared = slot_well >= 0
-    owner = jnp.sum(
-        jnp.where(slot_well[:, None] == jnp.arange(wells)[None, :], well_owner[None, :], 0), axis=1
-    )
-    home = shared & (owner == self_index)
-    away = shared & (owner != self_index)
-    bound = (owner[:, None] // tile_count == jnp.arange(sector_count)[None, :]) & away[:, None]
-    slots = slot_well.shape[0]
-    earlier = jnp.arange(slots)[None, :] < jnp.arange(slots)[:, None]
-    before = jnp.dot(
-        earlier.astype(jnp.bfloat16), bound.astype(jnp.bfloat16), preferred_element_type=jnp.float32
-    )
-    position = jnp.sum(jnp.where(bound, before, 0.0), axis=1).astype(jnp.int32)
-    place = jnp.where(away, owner // tile_count * CAP + position, -1)
-    return shared, home, place
+def outputs_kernel(
+    rates, duals, placing, matching, values, answers, roles, new_rates, new_duals, consensus
+):
+    ours = (((0,), (0,)), ((), ()))
+    added = lax.dot_general(matching[0], values[...], ours, preferred_element_type=jnp.float32)
+    from_peer = lax.dot_general(placing[0], answers[...], ours, preferred_element_type=jnp.float32)
+    scale, kind = roles[0, :, 0:1], roles[1, :, 0:1]
+    wide, kept = rates[0].astype(jnp.float32), duals[...]
+    offer = (wide + kept).astype(jnp.bfloat16).astype(jnp.float32)
+    mean = (2.0 * offer + added) * scale
+    agreed = jnp.where(kind > 1.5, mean, jnp.where(kind > 0.5, from_peer, wide))
+    new_rates[...] = rates[0]
+    consensus[...] = agreed
+    new_duals[...] = jnp.where(kind > 0.5, kept + wide - agreed, kept)
 
 
 def shards(rates, target, prior_consensus, duals, response, block_cols, slot_well, well_owner):
@@ -302,25 +323,23 @@
     width = periods // TILES
     rows = TILES * slots
     slabs = sectors * SLAB
-    shared, home, place = slot_roles(slot_well, well_owner, sectors, TILES)
-    shared, home = shared.astype(jnp.int32), home.astype(jnp.int32)
-    empty = jnp.zeros_like(place)
-    roles = jnp.stack([place, slot_well, home] + [empty] * 5)
-    role_cols = jnp.stack([home, shared], axis=1)
     cols = jnp.broadcast_to(block_cols.reshape(-1, 1), (block_cols.size, 128))
     bf16, f32, i32 = jnp.bfloat16, jnp.float32, jnp.int32
     whole = pl.BlockSpec(memory_space=pltpu.VMEM)
     far = pl.BlockSpec(memory_space=pl.ANY)
     dma = pltpu.SemaphoreType.DMA
-    return pl.pallas_call(
+    moved = pl.pallas_call(
         functools.partial(round_kernel, sectors),
         out_shape=(
-            jax.ShapeDtypeStruct((slots, periods), bf16),
-            jax.ShapeDtypeStruct((slots, periods), f32),
-            jax.ShapeDtypeStruct((slots, periods), f32),
+            jax.ShapeDtypeStruct((TILES, slots, width), bf16),
+            jax.ShapeDtypeStruct((TILES, slabs, slots), bf16),
+            jax.ShapeDtypeStruct((TILES, slabs, slots), bf16),
+            jax.ShapeDtypeStruct((slabs, width), bf16),
+            jax.ShapeDtypeStruct((slabs, width), bf16),
+            jax.ShapeDtypeStruct((2, slots, 128), f32),
         ),
         in_specs=[far] * 5 + [whole] * 3,
-        out_specs=(far, far, far),
+        out_specs=(far,) * 6,
         scratch_shapes=[
             pltpu.VMEM((rows, width), bf16),
             pltpu.VMEM((rows, width), bf16),
@@ -344,20 +363,37 @@
             pltpu.VMEM((slabs, width), bf16),
             pltpu.VMEM((slabs, width), bf16),
             pltpu.VMEM((slabs, width), bf16),
-            pltpu.VMEM((TILES, slots, width), f32),
-            pltpu.VMEM((TILES, slots, width), f32),
-            pltpu.VMEM((TILES, slots, width), f32),
+            pltpu.VMEM((2, slots, 128), f32),
             dma((5,)),
             dma((5, TILES)),
             dma((5, TILES)),
             dma((3, sectors)),
             dma((3, sectors)),
-            dma((12,)),
+            dma((9,)),
         ],
         compiler_params=pltpu.CompilerParams(
             collective_id=0, has_side_effects=True, vmem_limit_bytes=56 << 20
         ),
-    )(rates, target, prior_consensus, duals, response, cols, roles, role_cols)
+    )(rates, target, prior_consensus, duals, response, cols, slot_well.reshape(1, -1), well_owner.reshape(1, -1))
+    columns = pl.BlockSpec((slots, width), lambda q: (0, q))
+    picks = pl.BlockSpec((1, slabs, slots), lambda q: (q, 0, 0))
+    rows_sent = pl.BlockSpec((slabs, width), lambda q: (0, 0))
+    return pl.pallas_call(
+        outputs_kernel,
+        grid=(TILES,),
+        out_shape=(
+            jax.ShapeDtypeStruct((slots, periods), bf16),
+            jax.ShapeDtypeStruct((slots, periods), f32),
+            jax.ShapeDtypeStruct((slots, periods), f32),
+        ),
+        in_specs=[
+            pl.BlockSpec((1, slots, width), lambda q: (q, 0, 0)),
+            columns, picks, picks, rows_sent, rows_sent,
+            pl.BlockSpec((2, slots, 128), lambda q: (0, 0, 0)),
+        ],
+        out_specs=(columns, columns, columns),
+        compiler_params=pltpu.CompilerParams(vmem_limit_bytes=40 << 20),
+    )(moved[0], duals, *moved[1:])
 
 
 def solution(mesh):

time: 86.2 us -> 84.4 us (0.979)
  other arithmetic: 1.98 us -> 0 us
  Pallas kernels: 73.3 us -> 74.5 us
  local copies, waits for them, and re-layouts: 9.68 us -> 8.75 us
    pallas_call x0 -> x1, Pallas kernels: none -> 3.5 us  [shards(): pl.pallas_call(outputs_kernel, grid=(TILES,), out_shape=(jax.ShapeDtypeSt...]
    pallas_call x1, Pallas kernels: 73.3 us -> 71 us  [shards(): pl.pallas_call(functools.partial(round_kernel, sectors), out_shape=(jax.S...]
    another operation x4 -> x0, local copies, waits for them, and re-layouts: 2.17 us -> none  [the longest x3 1.31 us: shards(): roles = jnp.stack([place, slot_well, home] + [empty] * 5)]
    reshape x0 -> x1, local copies, waits for them, and re-layouts: none -> 1.3 us  [shards(): well_owner.reshape(1, -1)]
    reduce_sum x1 -> x0, other arithmetic: 1.24 us -> none  [slot_roles(): jnp.sum(jnp.where(slot_well[:, None] == jnp.arange(wells)[None, :], well_...]
    unnamed x7 -> x14, local copies, waits for them, and re-layouts: 6.08 us -> 6.02 us
where the time goes in v3:
time: 84.4 us; the launch traced here: 83.9 us
  Pallas kernels  74.5 us (88%)
  local copies, waits for them, and re-layouts  8.75 us (10%)
    pallas_call x1, Pallas kernels, shards(): pl.pallas_call(functools.partial(round_kernel, sectors), out_shape=(jax.S...  71 us
    unnamed x14, local copies, waits for them, and re-layouts  6.02 us
    pallas_call x1, Pallas kernels, shards(): pl.pallas_call(outputs_kernel, grid=(TILES,), out_shape=(jax.ShapeDtypeSt...  3.5 us

profile of v3, /device:TPU:0, one launch (start us, length us, event | category | flops | bytes accessed | tf_op | source)
XLA Modules:
  0.0 83.9 jit_solution(18129143665210747425)
XLA Ops:
  0.6 0.8 broadcast_in_dim.7
  1.4 1.3 %reshape.15.well_owner = s32[1,1536]{1,0:T(1,128)} reshape(s32[1536]{0:T(1024)} %param.15) | data formatting | bytes 12288 | tf_op jit(solution)/shard_map/reshape | solution.py:377
  2.7 0.7 broadcast_in_dim.8.cols
  3.4 0.0 copy-start
  3.4 71.0 %shard_map.103 = (bf16[4,512,256]{2,1,0:T(8,128)(2,1)}, bf16[4,128,512]{2,1,0:T(8,128)(2,1)}, bf16[4,128,512]{2,1,0:T(8,128)(2,1)}, bf16[128,256]{1,0:T(8,128)(2...) custom-call(bf16[512,1024]{1,0:T(8,128)(2,1)} %rates.1, bf16[512,1024]{1,0:T(8,128)(2,1)} %target.1, ...), custom_call_target="tpu_custom_call" | custom-call | tf_op jit(solution)/shard_map/pallas_call | solution.py:331
  74.4 0.0 copy-done
  74.4 0.0 copy-start.1
  74.4 1.2 %copy-done.1 = bf16[4,512,256]{2,1,0:T(8,128)(2,1)S(1)} copy-done((bf16[4,512,256]{2,1,0:T(8,128)(2,1)S(1)}, bf16[4,512,256]{2,1,0:T(8,128)(2,1)}, u32[]{:S(2)}) %copy-start.1) | copy-done | bytes 1048600
  75.6 0.0 copy-start.2
  75.6 1.0 %copy-done.2 = bf16[4,128,512]{2,1,0:T(8,128)(2,1)S(1)} copy-done((bf16[4,128,512]{2,1,0:T(8,128)(2,1)S(1)}, bf16[4,128,512]{2,1,0:T(8,128)(2,1)}, u32[]{:S(2)}) %copy-start.2) | copy-done | bytes 524312
  76.6 0.0 copy-start.3
  76.6 1.0 %copy-done.3 = bf16[4,128,512]{2,1,0:T(8,128)(2,1)S(1)} copy-done((bf16[4,128,512]{2,1,0:T(8,128)(2,1)S(1)}, bf16[4,128,512]{2,1,0:T(8,128)(2,1)}, u32[]{:S(2)}) %copy-start.3) | copy-done | bytes 524312
  77.7 0.0 copy-start.4
  77.7 1.0 %copy-done.4 = f32[2,512,128]{2,1,0:T(8,128)S(1)} copy-done((f32[2,512,128]{2,1,0:T(8,128)S(1)}, f32[2,512,128]{2,1,0:T(8,128)}, u32[]{:S(2)}) %copy-start.4) | copy-done | bytes 524312
  78.7 0.0 copy-start.5
  78.7 0.8 copy-done.5
  79.6 0.0 copy-start.6
  79.6 0.8 copy-done.6
  80.4 3.5 %shard_map.104 = (bf16[512,1024]{1,0:T(8,128)(2,1)}, f32[512,1024]{1,0:T(8,128)}, f32[512,1024]{1,0:T(8,128)}) custom-call(bf16[4,512,256]{2,1,0:T(8,128)(2,1)S(1)} %copy-done.1, f32[512,1024]{1,0:T(8,128)S(1)} %copy-done, bf16[4,128,512]{2,1,0:T(8,128)(2,1)S(1)} %copy-done.2, bf16[4,128,512]{2,1,0:T(8,128)(2,1)S(1)} %copy-done.3, ...), custom_call_target="tpu_custom_call" | custom-call | tf_op jit(solution)/shard_map/pallas_call | solution.py:381
Async XLA Ops:
  3.4 71.0 %copy-start = (f32[512,1024]{1,0:T(8,128)S(1)}, f32[512,1024]{1,0:T(8,128)}, u32[]{:S(2)}) copy-start(f32[512,1024]{1,0:T(8,128)} %duals.3) | copy-start | bytes 6291460
  74.4 1.2 %copy-start.1 = (bf16[4,512,256]{2,1,0:T(8,128)(2,1)S(1)}, bf16[4,512,256]{2,1,0:T(8,128)(2,1)}, u32[]{:S(2)}) copy-start(bf16[4,512,256]{2,1,0:T(8,128)(2,1)} %get-tuple-element.9.rates) | copy-start | bytes 3145732
  75.6 1.0 %copy-start.2 = (bf16[4,128,512]{2,1,0:T(8,128)(2,1)S(1)}, bf16[4,128,512]{2,1,0:T(8,128)(2,1)}, u32[]{:S(2)}) copy-start(bf16[4,128,512]{2,1,0:T(8,128)(2,1)} %get-tuple-element.10.placing) | copy-start | bytes 1572868
  76.6 1.0 %copy-start.3 = (bf16[4,128,512]{2,1,0:T(8,128)(2,1)S(1)}, bf16[4,128,512]{2,1,0:T(8,128)(2,1)}, u32[]{:S(2)}) copy-start(bf16[4,128,512]{2,1,0:T(8,128)(2,1)} %get-tuple-element.11.matching) | copy-start | bytes 1572868
  77.7 1.0 %copy-start.4 = (f32[2,512,128]{2,1,0:T(8,128)S(1)}, f32[2,512,128]{2,1,0:T(8,128)}, u32[]{:S(2)}) copy-start(f32[2,512,128]{2,1,0:T(8,128)} %get-tuple-element.14.roles) | copy-start | bytes 1572868
  78.7 0.8 %copy-start.5 = (bf16[128,256]{1,0:T(8,128)(2,1)S(1)}, bf16[128,256]{1,0:T(8,128)(2,1)}, u32[]{:S(2)}) copy-start(bf16[128,256]{1,0:T(8,128)(2,1)} %get-tuple-element.12.values) | copy-start | bytes 196612
  79.6 0.8 %copy-start.6 = (bf16[128,256]{1,0:T(8,128)(2,1)S(1)}, bf16[128,256]{1,0:T(8,128)(2,1)}, u32[]{:S(2)}) copy-start(bf16[128,256]{1,0:T(8,128)(2,1)} %get-tuple-element.13.answers) | copy-start | bytes 196612

commit v4 on v3

--- a/solution.py
+++ b/solution.py
@@ -392,7 +392,7 @@
             pl.BlockSpec((2, slots, 128), lambda q: (0, 0, 0)),
         ],
         out_specs=(columns, columns, columns),
-        compiler_params=pltpu.CompilerParams(vmem_limit_bytes=40 << 20),
+        compiler_params=pltpu.CompilerParams(vmem_limit_bytes=(64 << 20) - (64 << 10)),
     )(moved[0], duals, *moved[1:])
 
 

time: 84.4 us -> 80.5 us (0.954)
  local copies, waits for them, and re-layouts: 8.75 us -> 2.73 us
  Pallas kernels: 74.5 us -> 76.8 us
    unnamed x14 -> x0, local copies, waits for them, and re-layouts: 6.02 us -> none
    pallas_call x1, Pallas kernels: 3.5 us -> 6.02 us  [shards(): pl.pallas_call(outputs_kernel, grid=(TILES,), out_shape=(jax.ShapeDtypeSt...]
where the time goes in v4:
time: 80.5 us; the launch traced here: 80.2 us
  Pallas kernels  76.8 us (95%)
  local copies, waits for them, and re-layouts  2.73 us (3%)
    pallas_call x1, Pallas kernels, shards(): pl.pallas_call(functools.partial(round_kernel, sectors), out_shape=(jax.S...  70.8 us
    pallas_call x1, Pallas kernels, shards(): pl.pallas_call(outputs_kernel, grid=(TILES,), out_shape=(jax.ShapeDtypeSt...  6.02 us

profile of v4, /device:TPU:0, one launch (start us, length us, event | category | flops | bytes accessed | tf_op | source)
XLA Modules:
  0.0 80.2 jit_solution(17774456704714876249)
XLA Ops:
  0.6 0.8 broadcast_in_dim.7
  1.4 1.3 %reshape.15.well_owner = s32[1,1536]{1,0:T(1,128)} reshape(s32[1536]{0:T(1024)} %param.15) | data formatting | bytes 12288 | tf_op jit(solution)/shard_map/reshape | solution.py:377
  2.7 0.7 broadcast_in_dim.8.cols
  3.4 70.8 %shard_map.103 = (bf16[4,512,256]{2,1,0:T(8,128)(2,1)}, bf16[4,128,512]{2,1,0:T(8,128)(2,1)}, bf16[4,128,512]{2,1,0:T(8,128)(2,1)}, bf16[128,256]{1,0:T(8,128)(2...) custom-call(bf16[512,1024]{1,0:T(8,128)(2,1)} %rates.1, bf16[512,1024]{1,0:T(8,128)(2,1)} %target.1, ...), custom_call_target="tpu_custom_call" | custom-call | tf_op jit(solution)/shard_map/pallas_call | solution.py:331
  74.2 6.0 %shard_map.104 = (bf16[512,1024]{1,0:T(8,128)(2,1)}, f32[512,1024]{1,0:T(8,128)}, f32[512,1024]{1,0:T(8,128)}) custom-call(bf16[4,512,256]{2,1,0:T(8,128)(2,1)} %get-tuple-element.9.rates, f32[512,1024]{1,0:T(8,128)} %duals.3, bf16[4,128,512]{2,1,0:T(8,128)(2,1)} %get-tuple-element.10.placing, bf16[4,128,512]{2,1,0:T(8,128)(2,1)} %get-tuple-element.11.matching, ...), custom_call_target="tpu_custom_call" | custom-call | tf_op jit(solution)/shard_map/pallas_call | solution.py:381
